TPU v7x, 32 devices: a whole 2x2x4 slice. The times are simulated.
32 devices in a mesh: pole: 4 (over y, x), leaf: 8 (over z, core).
Axes of the slice: x: 2, y: 2, z: 4, core: 2. Of those that a mesh axis runs over, the one named last changes fastest.
Arguments:
- inverse_front: bfloat16 [4, 2, 8192, 8192], P('pole', None, 'leaf'), may hold values from -6 to 6
- factor_panel: bfloat16 [4, 8192, 512], P('pole', 'leaf'), may hold values from -0.0625 to 0.0625
- diag_inverse: bfloat16 [4, 256, 512], P('pole'), may hold values from -6 to 6
- pole_weight: float32 [4, 2], P('pole'), may hold values from -2.4 to 2.4
- structure: int32 [32], replicated, may hold values from 0 to 1, as said below
- block_owner: int32 [1024, 1], P('leaf'), may hold values from 0 to 7; in each aligned block of 128 rows (0 to 127, 128 to 255, ...) at most 32 rows name the same one
Outputs:
- owned_density: float32 [2048, 8, 256], P('leaf')
- diag_density: float32 [256, 256], replicated
Inputs may be any that keep to these rules, and one draw needn't show every extreme that they name: `structure`: exactly 16 entries are 1. `block_owner`: among the 128 blocks of one index of leaf no owner appears more than 32 times, and in some index's blocks one owner appears exactly 32 times.
All inputs are finite; a program needn't handle non-finite values.
Results may differ from a plain program's by a relative error of at most 0.0003.
Values may be sent and summed in bfloat16 or wider, within the bound.
A program may use at most 128 MiB of HBM per device.

v0:
```python
import jax
import jax.numpy as jnp
from jax import lax
from jax.sharding import PartitionSpec as P


def kept_rows(structure, first_row, row_count, block_width):
    block_ids = jnp.arange(structure.shape[0], dtype=jnp.int32)
    which_block = (first_row + jnp.arange(row_count, dtype=jnp.int32)) // block_width
    matches = which_block[:, None] == block_ids[None, :]
    return jnp.sum(jnp.where(matches, structure[None, :], 0), axis=1).astype(jnp.float32)


def panel_product(columns, panel):
    return jnp.einsum("pcrk,pkn->pcrn", columns, panel, preferred_element_type=jnp.float32)


def body(inverse_front, factor_panel, diag_inverse, pole_weight, structure, block_owner):
    leaves = lax.axis_size("leaf")
    rows_here = inverse_front.shape[2]
    block_width = factor_panel.shape[2] // 2
    first_row = lax.axis_index("leaf") * rows_here
    panel_rows = lax.all_gather(factor_panel, "leaf", axis=1, tiled=True)
    row_count = panel_rows.shape[1]
    keep_piece = kept_rows(structure, jnp.int32(0), row_count, block_width).astype(jnp.bfloat16)
    masked = panel_rows * keep_piece[None, :, None]
    product = panel_product(inverse_front, masked)
    keep_here = kept_rows(structure, first_row, rows_here, block_width)[None, :, None]
    block_real = -(product[:, 0, :, :block_width] - product[:, 1, :, block_width:]) * keep_here
    block_imag = -(product[:, 0, :, block_width:] + product[:, 1, :, :block_width]) * keep_here
    weight_real = pole_weight[:, 0][:, None, None]
    weight_imag = pole_weight[:, 1][:, None, None]
    density_part = jnp.sum(weight_real * block_imag + weight_imag * block_real, axis=0)
    panel_kept = factor_panel.astype(jnp.float32) * keep_here
    panel_real = panel_kept[:, :, :block_width]
    panel_imag = panel_kept[:, :, block_width:]
    precise = lax.Precision.HIGHEST

    def transposed(left_side, right_side):
        return jnp.einsum("prk,prn->pkn", left_side, right_side, precision=precise)

    schur_real = transposed(panel_real, block_real) - transposed(panel_imag, block_imag)
    schur_imag = transposed(panel_real, block_imag) + transposed(panel_imag, block_real)
    diag_full = diag_inverse.astype(jnp.float32)
    schur_real, schur_imag = lax.psum((schur_real, schur_imag), "leaf")
    corner_real = diag_full[:, :, :block_width] - schur_real
    corner_imag = diag_full[:, :, block_width:] - schur_imag
    corner_terms = jnp.sum(weight_real * corner_imag + weight_imag * corner_real, axis=0)
    diag_density = lax.psum(corner_terms, "pole")
    blocks_mine = block_owner.shape[0]
    element_rows = rows_here // blocks_mine
    capacity = max(2, (2 * blocks_mine + leaves - 1) // leaves)
    owners = block_owner[:, 0]
    one_hot = (owners[:, None] == jnp.arange(leaves, dtype=jnp.int32)[None, :]).astype(jnp.int32)
    ranks = jnp.sum((jnp.cumsum(one_hot, axis=0) - one_hot) * one_hot, axis=1)
    slot_index = owners * capacity + ranks
    density_rows = lax.psum(density_part, "pole")
    column_count = density_rows.shape[1]
    element_blocks = density_rows.reshape(blocks_mine, element_rows, column_count)
    buffer_zero = jnp.zeros((leaves * capacity, element_rows, column_count), jnp.float32)
    owned_density = lax.all_to_all(
        buffer_zero.at[slot_index].set(element_blocks),
        "leaf",
        split_axis=0,
        concat_axis=0,
        tiled=True,
    )
    return (owned_density, diag_density)


def solution(mesh):
    placed = (
        P("pole", None, "leaf", None),
        P("pole", "leaf", None),
        P("pole", None, None),
        P("pole", None),
        P(),
        P("leaf", None),
    )
    return jax.shard_map(
        body, mesh=mesh, in_specs=placed, out_specs=(P("leaf", None, None), P()), check_vma=False
    )
```

profile of v0, /device:TPU:0, one launch (start us, length us, event | category | flops | bytes accessed | tf_op | source)
XLA Modules:
  0.0 314.4 jit_solution(7714253229732450572)
XLA Ops:
  7.2 0.7 all-gather.2.cloned.1.call-update
  8.0 0.7 select_reduce_fusion.1
  8.7 1.0 convert_element_type.34
  9.7 1.3 fusion.43
  11.1 0.9 select_reduce_fusion
  12.0 1.4 convert_multiply_fusion
  13.4 81.0 %all-gather.2.cloned.1.call-done = bf16[1,8192,512]{2,1,0:T(8,128)(2,1)} async-done(((bf16[1,1024,512]{2,1,0:T(8,128)(2,1)}), bf16[1,8192,512]{2,1,0:T(8,128)(2,1)}) %all-gather.2.cloned.1.call-update) | async-done | bytes 8388624 | tf_op jit(solution)/shard_map/all_gather | solution.py:23
  94.4 24.1 %fusion.5 = f32[1,2,1024,512]{2,3,1,0:T(8,128)S(1)} fusion(bf16[1,2,1024,8192]{3,2,1,0:T(8,128)(2,1)} %param.6, bf16[1,8192,512]{2,1,0:T(8,128)(2,1)} %all-gather.2.cloned.1.call-done, bf16[8192]{0:T(1024)(128)(2,1)S(1)} %convert_convert_fusion), kind=kOutput, calls=%fused_computation.6 | convolution fusion | flops 17196646400 | bytes 46153728 | tf_op jit(solution)/shard_map/pcrk,pkn->pcrn/dot_general | solution.py:15
  118.5 1.9 fusion.14
  120.4 1.9 fusion.18
  122.4 2.6 fusion.10
  125.0 2.6 fusion.11
  127.7 3.9 %fusion.21 = f32[1024,256]{0,1:T(8,128)S(1)} fusion(f32[]{:T(128)} %bitcast.11, f32[1024]{0:T(1024)S(1)} %convert_element_type.33, f32[]{:T(128)} %bitcast.3, f32[1,2,1024,512]{2,3,1,0:T(8,128)} %copy-done), kind=kLoop, calls=%fused_computation.28 | loop fusion | flops 2359296 | bytes 5246984 | tf_op jit(solution)/shard_map/add | solution.py:33
  131.6 1.3 copy.13
  132.9 49.7 %all-reduce.5.cloned.1.call-done = (f32[1,256,256]{2,1,0:T(8,128)}, f32[1,256,256]{2,1,0:T(8,128)}) async-done(((f32[1,256,256]{2,1,0:T(8,128)}, f32[1,256,256]{2,1,0:T(8,128)}), (f32[1,256,256]{2,1,0:T(8,128)}, f32[1,256,256]{2,1,0:T(8,128)})) %all-reduce.5.cloned.1.call-update) | async-done | bytes 524304 | tf_op jit(solution)/shard_map/psum | solution.py:45
  182.6 3.0 fusion.29
  185.7 0.2 reduce_window_sum.11
  185.9 0.2 select_reduce_fusion.2
  186.1 56.3 %all-reduce.7.cloned.1.call-done = (f32[128,8,256]{2,1,0:T(8,128)}, f32[256,256]{1,0:T(8,128)}) async-done(((f32[128,8,256]{2,1,0:T(8,128)}, f32[256,256]{1,0:T(8,128)}), (f32[128,8,256]{2,1,0:T(8,128)}, f32[256,256]{1,0:T(8,128)})) %all-reduce.7.cloned.1.call-update) | async-done | bytes 1310736 | tf_op jit(solution)/shard_map/psum | solution.py:57
  242.4 0.1 broadcast_in_dim.26
  242.5 9.7 %scatter_fusion = f32[256,8,256]{2,1,0:T(8,128)S(1)} fusion(f32[256,8,256]{2,1,0:T(8,128)S(1)} %broadcast_in_dim.26, s32[128]{0:T(128)S(1)} %fusion.38, f32[128,8,256]{2,1,0:T(8,128)} %get-tuple-element.4), kind=kCustom, calls=%fused_computation | custom fusion | bytes 3146240 | tf_op jit(solution)/shard_map/scatter | solution.py:62
  252.3 53.6 %all_to_all.5 = f32[256,8,256]{2,1,0:T(8,128)S(1)} all-to-all(f32[256,8,256]{2,1,0:T(8,128)S(1)} %scatter_fusion), channel_id=1, replica_groups=mesh['pole'=4,'leaf'=8] {'leaf'}, dimensions={0} | all-to-all | bytes 4194304 | tf_op jit(solution)/shard_map/all_to_all | solution.py:61
  305.9 1.3 copy.22
  307.2 0.7 copy.23
  (17 shorter events, 0.3 us)
Async XLA Ops:
  7.2 87.2 %all-gather.2.cloned.1.call-start = ((), (), s32[]{:S(2)}) async-start(), calls=%async_computation.1 | async-start | bytes 9437184 | tf_op jit(solution)/shard_map/all_gather | solution.py:23
  7.9 174.7 %all-reduce.5.cloned.1.call-start = ((), (), s32[]{:S(2)}) async-start(), calls=%async_computation.2 | async-start | bytes 1048576 | tf_op jit(solution)/shard_map/psum | solution.py:45
  118.5 6.5 %copy-start = (f32[1,2,1024,512]{2,3,1,0:T(8,128)}, f32[1,2,1024,512]{2,3,1,0:T(8,128)S(1)}, u32[]{:S(2)}) copy-start(f32[1,2,1024,512]{2,3,1,0:T(8,128)S(1)} %fusion.5) | copy-start | bytes 12582916
  127.7 114.7 %all-reduce.7.cloned.1.call-start = ((), (), s32[]{:S(2)}) async-start(), calls=%async_computation.3 | async-start | bytes 2621440 | tf_op jit(solution)/shard_map/psum | solution.py:57
  127.7 57.9 %copy-start.2 = (s32[128,1]{0,1:T(1,128)S(1)}, s32[128,1]{0,1:T(1,128)}, u32[]{:S(2)}) copy-start(s32[128,1]{0,1:T(1,128)} %param.11) | copy-start | bytes 1540
  252.3 54.9 %copy-start.1 = (f32[256,256]{1,0:T(8,128)S(1)}, f32[256,256]{1,0:T(8,128)}, u32[]{:S(2)}) copy-start(f32[256,256]{1,0:T(8,128)} %get-tuple-element.11) | copy-start | bytes 786436
Sparse Core Ops, SparseCore 0:
  9.6 84.7 all-gather.1
  127.8 54.7 all-reduce.4
  186.6 55.7 all-reduce.6
where the time goes:
time: 315 us; the launch traced here: 314 us
  waiting for transfers between devices  188 us (60%)
  blocking collectives  53.6 us (17%)
  matrix products  33.2 us (11%)
  local copies, waits for them, and re-layouts  14.5 us (5%)
  between operations  13.9 us (4%)
  other arithmetic  11.4 us (4%)
    all_gather x1, waiting for transfers between devices, body(): panel_rows = lax.all_gather(factor_panel, 'leaf', axis=1, tiled=True)  81 us
    psum x1, waiting for transfers between devices, body(): density_rows = lax.psum(density_part, 'pole')  56.3 us
    all_to_all x1, blocking collectives, body(): lax.all_to_all(buffer_zero.at[slot_index].set(element_blocks), 'leaf', sp...  53.6 us
    psum x1, waiting for transfers between devices, body(): schur_real, schur_imag = lax.psum((schur_real, schur_imag), 'leaf')  49.7 us
    dot_general x1, matrix products, panel_product(): jnp.einsum('pcrk,pkn->pcrn', columns, panel, preferred_element_type=jnp.f...  24.1 us
    scatter x1, local copies, waits for them, and re-layouts, body(): buffer_zero.at[slot_index].set(element_blocks)  9.71 us
    dot_general x4, matrix products, transposed(): return jnp.einsum('prk,prn->pkn', left_side, right_side, precision=precise)  9.11 us
  transfers between devices with their start and end apart: 3, of which 3 were waited for; matrix products, arithmetic and copies ran while one was open for 4% of the time, Pallas kernels for 0%

commit v1 on v0

v1 whole, which is shorter than its diff:
```python
import jax
import jax.numpy as jnp
from jax import lax
from jax.sharding import PartitionSpec as P


def body(inverse_front, factor_panel, diag_inverse, pole_weight, structure, block_owner):
    leaves = lax.axis_size("leaf")
    poles = lax.axis_size("pole")
    rows_here = inverse_front.shape[2]
    order = inverse_front.shape[3]
    width = factor_panel.shape[2] // 2
    rows_per = order // structure.shape[0]
    first_row = lax.axis_index("leaf") * rows_here
    panel = lax.all_gather(factor_panel[0], "leaf", axis=0, tiled=True)
    keep_all = jnp.repeat(structure, rows_per)
    keep_here = lax.dynamic_slice(keep_all, (first_row,), (rows_here,)).astype(jnp.float32)[:, None]
    masked = panel * keep_all.astype(jnp.bfloat16)[:, None]
    real = jnp.dot(inverse_front[0, 0], masked, preferred_element_type=jnp.float32)
    imag = jnp.dot(inverse_front[0, 1], masked, preferred_element_type=jnp.float32)
    block_real = -(real[:, :width] - imag[:, width:]) * keep_here
    block_imag = -(real[:, width:] + imag[:, :width]) * keep_here
    wr = pole_weight[0, 0]
    wi = pole_weight[0, 1]
    im_part = wr * block_imag + wi * block_real
    re_part = wr * block_real - wi * block_imag
    both = jnp.concatenate([im_part, re_part], axis=0)
    left = jnp.concatenate([factor_panel[0, :, :width], factor_panel[0, :, width:]], axis=0)
    rounded = lax.reduce_precision(both, 8, 7)
    high = rounded.astype(jnp.bfloat16)
    low = (both - rounded).astype(jnp.bfloat16)
    contract = (((0,), (0,)), ((), ()))
    corner = lax.dot_general(left, high, contract, preferred_element_type=jnp.float32)
    corner += lax.dot_general(left, low, contract, preferred_element_type=jnp.float32)
    diag = diag_inverse[0].astype(jnp.float32)
    diag = wr * diag[:, width:] + wi * diag[:, :width]
    diag = jnp.where(lax.axis_index("leaf") == 0, diag, 0.0)
    diag_density = lax.psum(diag - corner, ("pole", "leaf"))

    blocks = block_owner.shape[0]
    element_rows = rows_here // blocks
    capacity = max(2, (2 * blocks + leaves - 1) // leaves)
    piece = element_rows // poles * width
    pieces = im_part.reshape(blocks, poles, piece).transpose(1, 0, 2)
    mine = lax.psum_scatter(pieces, "pole", scatter_dimension=0, tiled=True)[0]
    owners = block_owner[:, 0]
    at = jnp.arange(blocks, dtype=jnp.int32)
    earlier = (owners[None, :] == owners[:, None]) & (at[None, :] < at[:, None])
    slot = owners * capacity + jnp.sum(earlier.astype(jnp.int32), axis=1)
    sent = jnp.zeros((leaves * capacity, piece), jnp.float32).at[slot].set(mine)
    got = lax.all_to_all(sent, "leaf", split_axis=0, concat_axis=0, tiled=True)
    full = lax.all_gather(got, "pole", axis=0)
    owned = full.transpose(1, 0, 2).reshape(leaves * capacity, element_rows, width)
    return owned, diag_density


def solution(mesh):
    placed = (
        P("pole", None, "leaf", None),
        P("pole", "leaf", None),
        P("pole", None, None),
        P("pole", None),
        P(),
        P("leaf", None),
    )
    return jax.shard_map(
        body, mesh=mesh, in_specs=placed, out_specs=(P("leaf", None, None), P()), check_vma=False
    )
```

time: 315 us -> 350 us (1.11)
  waiting for transfers between devices: 188 us -> 269 us
  blocking collectives: 53.6 us -> 19.9 us
  other arithmetic: 11.4 us -> 2.9 us
    all_to_all x1, blocking collectives: 53.6 us -> 19.9 us  [body(): got = lax.all_to_all(sent, 'leaf', split_axis=0, concat_axis=0, tiled=True)]
    all_gather x1 -> x2, waiting for transfers between devices: 81 us -> 114 us  [the longest x1 85 us: body(): panel = lax.all_gather(factor_panel[0], 'leaf', axis=0, tiled=True)]
    unnamed x3 -> x5, waiting for transfers between devices: 0.71 us -> 26.9 us
    psum x2 -> x1, waiting for transfers between devices: 106 us -> 128 us  [body(): diag_density = lax.psum(diag - corner, ('pole', 'leaf'))]
    scatter x1, local copies, waits for them, and re-layouts: 9.71 us -> 1.57 us  [body(): sent = jnp.zeros((leaves * capacity, piece), jnp.float32).at[slot].set(mine)]
    reduce_sum x4 -> x1, other arithmetic: 4.81 us -> 0.17 us  [body(): slot = owners * capacity + jnp.sum(earlier.astype(jnp.int32), axis=1)]
    add x1 -> x0, other arithmetic: 3.85 us -> none  [body(): weight_real * block_imag + weight_imag * block_real]
    dot_general x5 -> x4, matrix products: 33.2 us -> 31.7 us  [the longest x1 14.4 us: body(): jnp.dot(inverse_front[0, 1], masked, preferred_element_type=jnp.float32)]
  transfers between devices with their start and end apart: 3 -> 4, of which waited for: 3 -> 4; matrix products, arithmetic and copies ran while one was open for 4% -> 2% of each run, Pallas kernels for 0% -> 0%
where the time goes in v1:
time: 350 us; the launch traced here: 349 us
  waiting for transfers between devices  269 us (77%)
  matrix products  31.7 us (9%)
  blocking collectives  19.9 us (6%)
  between operations  13.9 us (4%)
  local copies, waits for them, and re-layouts  11.7 us (3%)
    psum x1, waiting for transfers between devices, body(): diag_density = lax.psum(diag - corner, ('pole', 'leaf'))  128 us
    all_gather x1, waiting for transfers between devices, body(): panel = lax.all_gather(factor_panel[0], 'leaf', axis=0, tiled=True)  85 us
    all_gather x1, waiting for transfers between devices, body(): full = lax.all_gather(got, 'pole', axis=0)  29.3 us
    unnamed x5, waiting for transfers between devices  26.9 us
    all_to_all x1, blocking collectives, body(): got = lax.all_to_all(sent, 'leaf', split_axis=0, concat_axis=0, tiled=True)  19.9 us
    dot_general x1, matrix products, body(): jnp.dot(inverse_front[0, 1], masked, preferred_element_type=jnp.float32)  14.4 us
    dot_general x1, matrix products, body(): jnp.dot(inverse_front[0, 0], masked, preferred_element_type=jnp.float32)  14.4 us
  transfers between devices with their start and end apart: 4, of which 4 were waited for; matrix products, arithmetic and copies ran while one was open for 2% of the time, Pallas kernels for 0%

profile of v1, /device:TPU:0, one launch (start us, length us, event | category | flops | bytes accessed | tf_op | source)
XLA Modules:
  0.0 349.4 jit_solution(12021330932918548318)
XLA Ops:
  7.2 0.7 all-gather.6.cloned.1.call-update
  8.0 0.1 broadcast_bitcast_fusion
  8.1 1.3 fusion.33
  9.4 85.0 %all-gather.6.cloned.1.call-done = bf16[1,8192,512]{2,1,0:T(8,128)(2,1)} async-done(((bf16[1,1024,512]{2,1,0:T(8,128)(2,1)}), bf16[1,8192,512]{2,1,0:T(8,128)(2,1)}) %all-gather.6.cloned.1.call-update) | async-done | bytes 8388624 | tf_op jit(solution)/shard_map/all_gather | solution.py:15
  94.4 14.4 %fusion.12 = f32[1024,512]{0,1:T(8,128)S(1)} fusion(bf16[1,2,1024,8192]{3,2,1,0:T(8,128)(2,1)} %param.6, bf16[1,8192,512]{2,1,0:T(8,128)(2,1)} %all-gather.6.cloned.1.call-done, bf16[8192]{0:T(1024)(128)(2,1)S(1)} %convert_element_type.26), kind=kOutput, calls=%fused_computation.15 | convolution fusion | flops 8594128896 | bytes 27279360 | tf_op jit(solution)/shard_map/dot_general | solution.py:20
  108.8 14.4 %fusion.9 = f32[1024,512]{0,1:T(8,128)S(1)} fusion(bf16[1,2,1024,8192]{3,2,1,0:T(8,128)(2,1)} %param.6, bf16[1,8192,512]{2,1,0:T(8,128)(2,1)S(1)} %copy-done.4, bf16[8192]{0:T(1024)(128)(2,1)S(1)} %convert_element_type.26), kind=kOutput, calls=%fused_computation.14 | convolution fusion | flops 8594128896 | bytes 27279360 | tf_op jit(solution)/shard_map/dot_general | solution.py:19
  123.3 2.7 multiply_subtract_fusion
  125.9 0.3 copy.15
  126.3 0.5 reshape.27
  126.8 1.3 copy.16
  128.2 0.2 convert_reduce_fusion
  128.3 26.1 %reduce-scatter.4.cloned.1.call-done = f32[1,128,512]{2,1,0:T(8,128)} async-done(((f32[4,128,512]{2,1,0:T(8,128)}), f32[1,128,512]{2,1,0:T(8,128)}) %reduce-scatter.4.cloned.1.call-update) | async-done | bytes 262160
  154.5 1.6 scatter_custom_fusion
  156.1 19.9 %all_to_all.9 = f32[8,32,512]{2,1,0:T(8,128)} all-to-all(f32[8,32,512]{2,1,0:T(8,128)S(1)} %bitcast.54), channel_id=1, replica_groups=mesh['pole'=4,'leaf'=8] {'leaf'}, dimensions={0} | all-to-all | bytes 1048576 | tf_op jit(solution)/shard_map/all_to_all | solution.py:51
  176.0 0.1 bitcast_convert_fusion
  176.1 0.1 slice_bitcast_fusion.1
  176.2 1.0 copy-done.2
  177.2 0.5 fusion.17
  177.7 2.4 fusion.15
  180.1 29.3 %all-gather.4.cloned.1.call-done = f32[4,256,512]{2,1,0:T(8,128)} async-done(((f32[1,256,512]{2,1,0:T(8,128)}), f32[4,256,512]{2,1,0:T(8,128)}) %all-gather.4.cloned.1.call-update) | async-done | bytes 2097168 | tf_op jit(solution)/shard_map/all_gather | solution.py:52
  209.4 1.9 copy.17
  211.3 2.0 copy.18
  213.3 127.9 %all-reduce.3.cloned.1.call-done = f32[256,256]{1,0:T(8,128)} async-done(((f32[256,256]{1,0:T(8,128)}), f32[256,256]{1,0:T(8,128)}) %all-reduce.3.cloned.1.call-update) | async-done | bytes 262160 | tf_op jit(solution)/shard_map/psum | solution.py:38
  341.2 1.7 copy.21
  (22 shorter events, 0.3 us)
Async XLA Ops:
  7.2 0.8 copy-start
  7.2 87.2 %all-gather.6.cloned.1.call-start = ((), (), s32[]{:S(2)}) async-start(), calls=%async_computation.4 | async-start | bytes 9437184 | tf_op jit(solution)/shard_map/all_gather | solution.py:15
  7.9 146.6 %reduce-scatter.4.cloned.1.call-start = ((), (), s32[]{:S(2)}) async-start(), calls=%async_computation.5 | async-start | bytes 1310720
  94.4 14.4 %copy-start.4 = (bf16[1,8192,512]{2,1,0:T(8,128)(2,1)S(1)}, bf16[1,8192,512]{2,1,0:T(8,128)(2,1)}, u32[]{:S(2)}) copy-start(bf16[1,8192,512]{2,1,0:T(8,128)(2,1)} %all-gather.6.cloned.1.call-done) | copy-start | bytes 25165828
  126.8 1.4 copy-start.5
  128.1 48.0 %copy-start.3 = (bf16[1,256,512]{2,1,0:T(8,128)(2,1)S(1)}, bf16[1,256,512]{2,1,0:T(8,128)(2,1)}, u32[]{:S(2)}) copy-start(bf16[1,256,512]{2,1,0:T(8,128)(2,1)} %param.8) | copy-start | bytes 786436
  128.1 48.0 %copy-start.1 = (bf16[1,1024,512]{2,1,0:T(8,128)(2,1)S(1)}, bf16[1,1024,512]{2,1,0:T(8,128)(2,1)}, u32[]{:S(2)}) copy-start(bf16[1,1024,512]{2,1,0:T(8,128)(2,1)} %param.7) | copy-start | bytes 3145732
  128.1 81.3 %all-gather.4.cloned.1.call-start = ((), (), s32[]{:S(2)}) async-start(), calls=%async_computation.2 | async-start | bytes 2621440 | tf_op jit(solution)/shard_map/all_gather | solution.py:52
  175.9 1.2 copy-start.2
  176.0 165.2 %all-reduce.3.cloned.1.call-start = ((), (), s32[]{:S(2)}) async-start(), calls=%async_computation.3 | async-start | bytes 524288 | tf_op jit(solution)/shard_map/psum | solution.py:38
Sparse Core Ops, SparseCore 0:
  9.6 84.7 all-gather.5
  128.2 26.2 reduce-scatter.3
  176.1 33.2 all-gather.3
  216.2 124.9 all-reduce.2

commit v2 on v1

v2 whole, which is shorter than its diff:
```python
import functools
import jax
import jax.numpy as jnp
from jax import lax
from jax.experimental import pallas as pl
from jax.experimental.pallas import tpu as pltpu
from jax.sharding import PartitionSpec as P

CHUNKS = 1


def product_kernel(group, steps, kept, bands, rows_per, width, ids, weight, *refs):
    fronts = refs[:group]
    panels = refs[group : 2 * group]
    local, density, corner, total = refs[2 * group :]
    step = pl.program_id(0)
    transposed = (((0,), (0,)), ((), ()))

    @pl.when(step == 0)
    def _():
        corner[...] = jnp.zeros_like(corner)

    for band in range(bands):
        rows = pl.ds(band * rows_per, rows_per)
        used = ids[kept + band] == 1

        @pl.when(used)
        def _():
            for part in range(2):
                value = jnp.dot(fronts[0][0, part, rows], panels[0][...], preferred_element_type=jnp.float32)
                for g in range(1, group):
                    value += jnp.dot(fronts[g][0, part, rows], panels[g][...], preferred_element_type=jnp.float32)

                @pl.when(step == 0)
                def _():
                    total[part, rows] = value

                @pl.when(step > 0)
                def _():
                    total[part, rows] += value

        @pl.when(used & (step == steps - 1))
        def _():
            block_real = total[1, rows, width:] - total[0, rows, :width]
            block_imag = -(total[0, rows, width:] + total[1, rows, :width])
            wr = weight[0]
            wi = weight[1]
            im_part = wr * block_imag + wi * block_real
            re_part = wr * block_real - wi * block_imag
            density[rows] = im_part
            for left, right in ((local[0, rows, :width], im_part), (local[0, rows, width:], re_part)):
                high = right.astype(jnp.bfloat16)
                low = (right - high.astype(jnp.float32)).astype(jnp.bfloat16)
                corner[...] += lax.dot_general(left, high, transposed, preferred_element_type=jnp.float32)
                corner[...] += lax.dot_general(left, low, transposed, preferred_element_type=jnp.float32)

        @pl.when(jnp.logical_not(used) & (step == steps - 1))
        def _():
            density[rows] = jnp.zeros((rows_per, width), jnp.float32)


def product(ids, weight, front, panel, local, kept, rows_per):
    rows_here = front.shape[2]
    width = local.shape[2] // 2
    group = next(g for g in (4, 2, 1) if kept % g == 0)
    steps = kept // group
    bands = rows_here // rows_per

    def front_at(g, k, ids, weight):
        return (0, 0, 0, ids[k * group + g])

    def panel_at(g, k, ids, weight):
        return (ids[k * group + g], 0)

    in_specs = [
        pl.BlockSpec((1, 2, rows_here, rows_per), functools.partial(front_at, g)) for g in range(group)
    ]
    in_specs += [pl.BlockSpec((rows_per, 2 * width), functools.partial(panel_at, g)) for g in range(group)]
    in_specs.append(pl.BlockSpec((1, rows_here, 2 * width), lambda k, ids, weight: (0, 0, 0)))
    flops = 2 * 2 * rows_here * kept * rows_per * 2 * width
    return pl.pallas_call(
        functools.partial(product_kernel, group, steps, kept, bands, rows_per, width),
        out_shape=(
            jax.ShapeDtypeStruct((rows_here, width), jnp.float32),
            jax.ShapeDtypeStruct((width, width), jnp.float32),
        ),
        grid_spec=pltpu.PrefetchScalarGridSpec(
            num_scalar_prefetch=2,
            grid=(steps,),
            in_specs=in_specs,
            out_specs=(
                pl.BlockSpec((rows_here, width), lambda k, ids, weight: (0, 0)),
                pl.BlockSpec((width, width), lambda k, ids, weight: (0, 0)),
            ),
            scratch_shapes=[pltpu.VMEM((2, rows_here, 2 * width), jnp.float32)],
        ),
        compiler_params=pltpu.CompilerParams(vmem_limit_bytes=44 << 20),
        cost_estimate=pl.CostEstimate(
            flops=flops, bytes_accessed=4 * rows_here * kept * rows_per, transcendentals=0
        ),
    )(ids, weight, *([front] * group), *([panel] * group), local)


def body(inverse_front, factor_panel, diag_inverse, pole_weight, structure, block_owner):
    leaves = lax.axis_size("leaf")
    poles = lax.axis_size("pole")
    leaf = lax.axis_index("leaf")
    rows_here = inverse_front.shape[2]
    width = factor_panel.shape[2] // 2
    bands_all = structure.shape[0]
    rows_per = inverse_front.shape[3] // bands_all
    bands = rows_here // rows_per
    kept = bands_all // 2
    panel = lax.all_gather(factor_panel[0], "leaf", axis=0, tiled=True)

    band = jnp.arange(bands_all, dtype=jnp.int32)
    before = jnp.sum(jnp.where(band[None, :] < band[:, None], structure[None, :], 0), axis=1)
    hit = (before[None, :] == jnp.arange(kept, dtype=jnp.int32)[:, None]) & (structure[None, :] == 1)
    chosen = jnp.sum(jnp.where(hit, band[None, :], 0), axis=1)
    flags = lax.dynamic_slice(structure, (leaf * bands,), (bands,))
    ids = jnp.concatenate([chosen, flags]).astype(jnp.int32)
    density, corner = product(ids, pole_weight[0], inverse_front, panel, factor_panel, kept, rows_per)

    diag = diag_inverse[0].astype(jnp.float32)
    diag = pole_weight[0, 0] * diag[:, width:] + pole_weight[0, 1] * diag[:, :width]
    corner = jnp.where(leaf == 0, diag, 0.0) - corner

    blocks = block_owner.shape[0]
    element_rows = rows_here // blocks
    capacity = max(2, (2 * blocks + leaves - 1) // leaves)
    piece = element_rows // poles * width
    pieces = density.reshape(blocks, poles, piece).transpose(1, 0, 2)
    corners = corner.reshape(poles, -1, piece)
    owners = block_owner[:, 0]
    at = jnp.arange(blocks, dtype=jnp.int32)
    earlier = (owners[None, :] == owners[:, None]) & (at[None, :] < at[:, None])
    slot = owners * capacity + jnp.sum(earlier.astype(jnp.int32), axis=1)
    parts = []
    for chunk in range(CHUNKS):
        share = piece // CHUNKS
        some = pieces[:, :, chunk * share : (chunk + 1) * share]
        mine = lax.psum_scatter(some, "pole", scatter_dimension=0, tiled=True)[0]
        corner_some = corners[:, :, chunk * share : (chunk + 1) * share]
        corner_one = lax.psum_scatter(corner_some, "pole", scatter_dimension=0, tiled=True)
        corner_mine = jnp.sum(lax.all_gather(corner_one[0], "leaf", axis=0), axis=0)
        sent = jnp.zeros((leaves * capacity, share), jnp.float32).at[slot].set(mine)
        got = lax.all_to_all(sent, "leaf", split_axis=0, concat_axis=0, tiled=True)
        parts.append(lax.all_gather(jnp.concatenate([got, corner_mine], axis=0), "pole", axis=0))
    full = parts[0] if CHUNKS == 1 else jnp.concatenate(parts, axis=2)
    slots = leaves * capacity
    owned = full[:, :slots].transpose(1, 0, 2).reshape(slots, element_rows, width)
    return owned, full[:, slots:].reshape(width, width)


def solution(mesh):
    placed = (
        P("pole", None, "leaf", None),
        P("pole", "leaf", None),
        P("pole", None, None),
        P("pole", None),
        P(),
        P("leaf", None),
    )
    return jax.shard_map(
        body, mesh=mesh, in_specs=placed, out_specs=(P("leaf", None, None), P()), check_vma=False
    )
```

time: 350 us -> 246 us (0.70)
  waiting for transfers between devices: 269 us -> 186 us
  matrix products: 31.7 us -> 0 us
  Pallas kernels: 0 us -> 9.93 us
  blocking collectives: 19.9 us -> 14.9 us
  starting transfers between devices: 0.16 us -> 4.77 us
    psum x1 -> x0, waiting for transfers between devices: 128 us -> none  [body(): diag_density = lax.psum(diag - corner, ('pole', 'leaf'))]
    unnamed x5 -> x6, waiting for transfers between devices: 26.9 us -> 63.6 us
    dot_general x4 -> x0, matrix products: 31.7 us -> none  [the longest x1 14.4 us: body(): jnp.dot(inverse_front[0, 1], masked, preferred_element_type=jnp.float32)]
    all_to_all x1 -> x0, blocking collectives: 19.9 us -> none  [body(): got = lax.all_to_all(sent, 'leaf', split_axis=0, concat_axis=0, tiled=True)]
    all_gather x0 -> x1, blocking collectives: none -> 14.9 us  [body(): corner_mine = jnp.sum(lax.all_gather(corner_one[0], 'leaf', axis=0), axis=0)]
    pallas_call x0 -> x1, Pallas kernels: none -> 9.93 us  [product(): pl.pallas_call(functools.partial(product_kernel, group, steps, kept, band...]
    all_gather x1, waiting for transfers between devices: 29.3 us -> 37.9 us  [body(): lax.all_gather(jnp.concatenate([got, corner_mine], axis=0), 'pole', axis=0)]
    reshape x1 -> x5, local copies, waits for them, and re-layouts: 0.5 us -> 5.15 us  [the longest x1 1.84 us: body(): full[:, :slots].transpose(1, 0, 2).reshape(slots, element_rows, width)]
  transfers between devices with their start and end apart: 4 -> 5, of which waited for: 4 -> 4; matrix products, arithmetic and copies ran while one was open for 2% -> 2% of each run, Pallas kernels for 0% -> 0%
where the time goes in v2:
time: 246 us; the launch traced here: 248 us
  waiting for transfers between devices  186 us (76%)
  blocking collectives  14.9 us (6%)
  local copies, waits for them, and re-layouts  14.6 us (6%)
  between operations  13.9 us (6%)
  Pallas kernels  9.93 us (4%)
  starting transfers between devices  4.77 us (2%)
  other arithmetic  3.99 us (2%)
    all_gather x1, waiting for transfers between devices, body(): panel = lax.all_gather(factor_panel[0], 'leaf', axis=0, tiled=True)  84.1 us
    unnamed x6, waiting for transfers between devices  63.6 us
    all_gather x1, waiting for transfers between devices, body(): lax.all_gather(jnp.concatenate([got, corner_mine], axis=0), 'pole', axis=0)  37.9 us
    all_gather x1, blocking collectives, body(): corner_mine = jnp.sum(lax.all_gather(corner_one[0], 'leaf', axis=0), axis=0)  14.9 us
    pallas_call x1, Pallas kernels, product(): pl.pallas_call(functools.partial(product_kernel, group, steps, kept, band...  9.93 us
  transfers between devices with their start and end apart: 5, of which 4 were waited for; matrix products, arithmetic and copies ran while one was open for 2% of the time, Pallas kernels for 0%

profile of v2, /device:TPU:0, one launch (start us, length us, event | category | flops | bytes accessed | tf_op | source)
XLA Modules:
  0.0 247.7 jit_solution(9496615607843343767)
XLA Ops:
  7.2 0.7 all-gather.5.cloned.1.call-update
  7.9 0.7 dynamic_slice.3
  8.7 0.8 select_reduce_fusion
  9.4 0.7 broadcast_compare_fusion
  10.3 84.1 %all-gather.5.cloned.1.call-done = bf16[1,8192,512]{2,1,0:T(8,128)(2,1)} async-done(((bf16[1,1024,512]{2,1,0:T(8,128)(2,1)}), bf16[1,8192,512]{2,1,0:T(8,128)(2,1)}) %all-gather.5.cloned.1.call-update) | async-done | bytes 8388624 | tf_op jit(solution)/shard_map/all_gather | solution.py:114
  94.4 1.2 copy-done
  95.6 0.7 copy-done.1
  96.3 9.9 %shard_map.77 = (f32[1024,256]{1,0:T(8,128)S(1)}, f32[256,256]{1,0:T(8,128)S(1)}) custom-call(s32[20]{0:T(128)S(1)} %pad_add_fusion.ids, f32[2]{0:T(128)S(1)} %bitcast.26, bf16[1,2,1024,8192]{3,2,1,0:T(8,128)(2,1)} %refs_3_.1, bf16[1,2,1024,8192]{3,2,1,0:T(8,128)(2,1)} %refs_3_.1, bf16[1,2,1024,8192]{3,2,1,0:T(8,128)(2,1)} %refs_3_.1, ...), custom_call_target="tpu_custom_call" | custom-call | flops 8589934592 | bytes 16777216 | tf_op jit(solution)/shard_map/pallas_call | solution.py:81
  106.7 1.3 copy.14
  108.1 0.6 fusion.9
  108.9 36.1 %reduce-scatter.7.cloned.1.call-done = f32[1,128,512]{2,1,0:T(8,128)} async-done(((f32[4,128,512]{2,1,0:T(8,128)}), f32[1,128,512]{2,1,0:T(8,128)}) %reduce-scatter.7.cloned.1.call-update) | async-done | bytes 262160
  145.0 2.2 scatter_custom_fusion
  147.2 4.6 %all-to-all-start = ((f32[8,32,512]{2,1,0:T(8,128)}), f32[8,32,512]{2,1,0:T(8,128)S(1)}, u32[]{:S(2)}, u32[]{:S(2)}) async-start(f32[8,32,512]{2,1,0:T(8,128)} %bitcast.8), calls=%async_computation | async-start | bytes 1048576 | tf_op jit(solution)/shard_map/all_to_all | solution.py:147
  151.8 1.2 fusion.2
  153.1 0.8 reshape.27
  153.9 26.8 %reduce-scatter.9.cloned.1.call-done = f32[1,32,512]{2,1,0:T(8,128)} async-done(((f32[4,32,512]{2,1,0:T(8,128)}), f32[1,32,512]{2,1,0:T(8,128)}) %reduce-scatter.9.cloned.1.call-update) | async-done | bytes 65552
  180.8 14.9 %all_gather.13 = f32[8,32,512]{2,1,0:T(8,128)S(1)} all-gather(f32[1,32,512]{2,1,0:T(8,128)} %reduce-scatter.9.cloned.1.call-done), channel_id=1, replica_groups=mesh['pole'=4,'leaf'=8] {'leaf'}, dimensions={0}, use_global_device_ids=true | all-gather | bytes 589824 | tf_op jit(solution)/shard_map/all_gather | solution.py:145
  195.7 0.9 pad_maximum_fusion
  196.6 37.9 %all-gather.7.cloned.1.call-done = f32[1152,512]{1,0:T(8,128)} async-done(((f32[288,512]{1,0:T(8,128)}), f32[1152,512]{1,0:T(8,128)}) %all-gather.7.cloned.1.call-update) | async-done | bytes 2359312 | tf_op jit(solution)/shard_map/all_gather | solution.py:148
  234.5 1.8 slice_bitcast_fusion
  236.3 1.0 slice.27
  237.3 1.4 copy.12
  238.6 1.8 reshape.28
  240.5 0.7 reshape.29
  (23 shorter events, 1.2 us)
Async XLA Ops:
  7.2 87.2 %all-gather.5.cloned.1.call-start = ((), (), s32[]{:S(2)}) async-start(), calls=%async_computation.3 | async-start | bytes 9437184 | tf_op jit(solution)/shard_map/all_gather | solution.py:114
  7.9 137.1 %reduce-scatter.7.cloned.1.call-start = ((), (), s32[]{:S(2)}) async-start(), calls=%async_computation.5 | async-start | bytes 1310720
  94.4 1.2 copy-start
  95.6 0.7 copy-start.1
  106.2 1.9 copy-start.2
  106.2 2.4 copy-start.4
  106.2 2.6 %copy-start.3 = (bf16[1,256,512]{2,1,0:T(8,128)(2,1)S(1)}, bf16[1,256,512]{2,1,0:T(8,128)(2,1)}, u32[]{:S(2)}) copy-start(bf16[1,256,512]{2,1,0:T(8,128)(2,1)} %param.8) | copy-start | bytes 786436
  147.2 48.5 %all-to-all-start = ((f32[8,32,512]{2,1,0:T(8,128)}), f32[8,32,512]{2,1,0:T(8,128)S(1)}, u32[]{:S(2)}, u32[]{:S(2)}) async-start(f32[8,32,512]{2,1,0:T(8,128)} %bitcast.8), calls=%async_computation | async-start | bytes 1048576 | tf_op jit(solution)/shard_map/all_to_all | solution.py:147
  151.8 29.0 %reduce-scatter.9.cloned.1.call-start = ((), (), s32[]{:S(2)}) async-start(), calls=%async_computation.6 | async-start | bytes 327680
  153.9 80.6 %all-gather.7.cloned.1.call-start = ((), (), s32[]{:S(2)}) async-start(), calls=%async_computation.4 | async-start | bytes 2949120 | tf_op jit(solution)/shard_map/all_gather | solution.py:148
Sparse Core Ops, SparseCore 0:
  9.6 84.7 all-gather.4
  108.2 36.7 reduce-scatter.6
  156.2 24.5 reduce-scatter.8
  196.7 37.7 all-gather.6

commit v3 on v2

--- a/solution.py
+++ b/solution.py
@@ -130,7 +130,7 @@
     capacity = max(2, (2 * blocks + leaves - 1) // leaves)
     piece = element_rows // poles * width
     pieces = density.reshape(blocks, poles, piece).transpose(1, 0, 2)
-    corners = corner.reshape(poles, -1, piece)
+    pieces = jnp.concatenate([pieces, corner.reshape(poles, -1, piece)], axis=1)
     owners = block_owner[:, 0]
     at = jnp.arange(blocks, dtype=jnp.int32)
     earlier = (owners[None, :] == owners[:, None]) & (at[None, :] < at[:, None])
@@ -139,11 +139,9 @@
     for chunk in range(CHUNKS):
         share = piece // CHUNKS
         some = pieces[:, :, chunk * share : (chunk + 1) * share]
-        mine = lax.psum_scatter(some, "pole", scatter_dimension=0, tiled=True)[0]
-        corner_some = corners[:, :, chunk * share : (chunk + 1) * share]
-        corner_one = lax.psum_scatter(corner_some, "pole", scatter_dimension=0, tiled=True)
-        corner_mine = jnp.sum(lax.all_gather(corner_one[0], "leaf", axis=0), axis=0)
-        sent = jnp.zeros((leaves * capacity, share), jnp.float32).at[slot].set(mine)
+        mine = lax.psum_scatter(some.reshape(-1, share), "pole", scatter_dimension=0, tiled=True)
+        corner_mine = jnp.sum(lax.all_gather(mine[blocks:], "leaf", axis=0), axis=0)
+        sent = jnp.zeros((leaves * capacity, share), jnp.float32).at[slot].set(mine[:blocks])
         got = lax.all_to_all(sent, "leaf", split_axis=0, concat_axis=0, tiled=True)
         parts.append(lax.all_gather(jnp.concatenate([got, corner_mine], axis=0), "pole", axis=0))
     full = parts[0] if CHUNKS == 1 else jnp.concatenate(parts, axis=2)

time: 246 us -> 227 us (0.923); the launches traced: 248 us -> 225 us
  waiting for transfers between devices: 186 us -> 148 us
  blocking collectives: 14.9 us -> 22.1 us
  Pallas kernels: 9.93 us -> 16.4 us
    unnamed x6 -> x3, waiting for transfers between devices: 63.6 us -> 0.71 us
    reduce_scatter x0 -> x1, waiting for transfers between devices: none -> 27.8 us  [body(): lax.psum_scatter(some.reshape(-1, share), 'pole', scatter_dimension=0, ti...]
    all_gather x1, blocking collectives: 14.9 us -> 22.1 us  [body(): corner_mine = jnp.sum(lax.all_gather(mine[blocks:], 'leaf', axis=0), axis=0)]
    pallas_call x1, Pallas kernels: 9.93 us -> 16.4 us  [product(): pl.pallas_call(functools.partial(product_kernel, group, steps, kept, band...]
  transfers between devices with their start and end apart: 5 -> 4, of which waited for: 4 -> 3; matrix products, arithmetic and copies ran while one was open for 2% -> 3% of each run, Pallas kernels for 0% -> 0%
where the time goes in v3:
time: 227 us; the launch traced here: 225 us
  waiting for transfers between devices  148 us (65%)
  blocking collectives  22.1 us (10%)
  Pallas kernels  16.4 us (7%)
  between operations  13.9 us (6%)
  local copies, waits for them, and re-layouts  13.4 us (6%)
  other arithmetic  6.23 us (3%)
  starting transfers between devices  4.73 us (2%)
    all_gather x1, waiting for transfers between devices, body(): panel = lax.all_gather(factor_panel[0], 'leaf', axis=0, tiled=True)  81.8 us
    all_gather x1, waiting for transfers between devices, body(): lax.all_gather(jnp.concatenate([got, corner_mine], axis=0), 'pole', axis=0)  37.6 us
    reduce_scatter x1, waiting for transfers between devices, body(): lax.psum_scatter(some.reshape(-1, share), 'pole', scatter_dimension=0, ti...  27.8 us
    all_gather x1, blocking collectives, body(): corner_mine = jnp.sum(lax.all_gather(mine[blocks:], 'leaf', axis=0), axis=0)  22.1 us
    pallas_call x1, Pallas kernels, product(): pl.pallas_call(functools.partial(product_kernel, group, steps, kept, band...  16.4 us
    all_to_all x1, starting transfers between devices, body(): got = lax.all_to_all(sent, 'leaf', split_axis=0, concat_axis=0, tiled=True)  4.61 us
  transfers between devices with their start and end apart: 4, of which 3 were waited for; matrix products, arithmetic and copies ran while one was open for 3% of the time, Pallas kernels for 0%

profile of v3, /device:TPU:0, one launch (start us, length us, event | category | flops | bytes accessed | tf_op | source)
XLA Modules:
  0.0 224.6 jit_solution(16478265411397101391)
XLA Ops:
  7.2 0.7 all-gather.6.cloned.1.call-update
  8.0 0.7 dynamic_slice.3
  8.7 0.8 select_reduce_fusion
  9.5 0.7 broadcast_compare_fusion
  10.3 1.3 fusion.9
  11.6 1.0 bitcast_convert_fusion
  12.6 81.8 %all-gather.6.cloned.1.call-done = bf16[1,8192,512]{2,1,0:T(8,128)(2,1)} async-done(((bf16[1,1024,512]{2,1,0:T(8,128)(2,1)}), bf16[1,8192,512]{2,1,0:T(8,128)(2,1)}) %all-gather.6.cloned.1.call-update) | async-done | bytes 8388624 | tf_op jit(solution)/shard_map/all_gather | solution.py:114
  94.4 0.7 copy-done.1
  95.1 16.4 %shard_map.77 = (f32[1024,256]{1,0:T(8,128)S(1)}, f32[256,256]{1,0:T(8,128)S(1)}) custom-call(s32[20]{0:T(128)S(1)} %pad_add_fusion.ids, f32[2]{0:T(128)S(1)} %bitcast.24, bf16[1,2,1024,8192]{3,2,1,0:T(8,128)(2,1)} %refs_3_.1, bf16[1,2,1024,8192]{3,2,1,0:T(8,128)(2,1)} %refs_3_.1, bf16[1,2,1024,8192]{3,2,1,0:T(8,128)(2,1)} %refs_3_.1, ...), custom_call_target="tpu_custom_call" | custom-call | flops 8589934592 | bytes 16777216 | tf_op jit(solution)/shard_map/pallas_call | solution.py:81
  111.5 1.3 fusion.4
  112.9 0.5 reshape.29
  113.8 1.2 pad_maximum_fusion
  115.2 27.8 %reduce-scatter.2.cloned.1.call-done = f32[160,512]{1,0:T(8,128)} async-done(((f32[640,512]{1,0:T(8,128)}), f32[160,512]{1,0:T(8,128)}) %reduce-scatter.2.cloned.1.call-update) | async-done | bytes 327696 | tf_op jit(solution)/shard_map/reduce_scatter | solution.py:142
  143.0 2.2 scatter_custom_fusion
  145.2 4.6 %all-to-all-start = ((f32[8,32,512]{2,1,0:T(8,128)}), f32[8,32,512]{2,1,0:T(8,128)S(1)}, u32[]{:S(2)}, u32[]{:S(2)}) async-start(f32[8,32,512]{2,1,0:T(8,128)} %bitcast.11), calls=%async_computation.1 | async-start | bytes 1048576 | tf_op jit(solution)/shard_map/all_to_all | solution.py:145
  149.9 0.8 slice.35
  150.7 22.1 %all-gather.1 = f32[256,512]{1,0:T(8,128)S(1)} all-gather(f32[32,512]{1,0:T(8,128)S(1)} %slice.35), channel_id=3, replica_groups=mesh['pole'=4,'leaf'=8] {'leaf'}, dimensions={0}, use_global_device_ids=true | all-gather | bytes 589824 | tf_op jit(solution)/shard_map/all_gather | solution.py:143
  172.9 0.9 pad_maximum_fusion.1
  173.7 37.6 %all-gather.8.cloned.1.call-done = f32[1152,512]{1,0:T(8,128)} async-done(((f32[288,512]{1,0:T(8,128)}), f32[1152,512]{1,0:T(8,128)}) %all-gather.8.cloned.1.call-update) | async-done | bytes 2359312 | tf_op jit(solution)/shard_map/all_gather | solution.py:146
  211.4 1.8 slice_bitcast_fusion
  213.1 1.0 slice.37
  214.1 1.4 copy.13
  215.5 1.8 reshape.32
  217.3 0.7 reshape.33
  (18 shorter events, 1.0 us)
Async XLA Ops:
  7.2 87.2 %copy-start = (bf16[1,1024,512]{2,1,0:T(8,128)(2,1)S(1)}, bf16[1,1024,512]{2,1,0:T(8,128)(2,1)}, u32[]{:S(2)}) copy-start(bf16[1,1024,512]{2,1,0:T(8,128)(2,1)} %refs_8_.1) | copy-start | bytes 3145732
  7.2 87.2 %all-gather.6.cloned.1.call-start = ((), (), s32[]{:S(2)}) async-start(), calls=%async_computation.3 | async-start | bytes 9437184 | tf_op jit(solution)/shard_map/all_gather | solution.py:114
  7.9 135.1 %reduce-scatter.2.cloned.1.call-start = ((), (), s32[]{:S(2)}) async-start(), calls=%async_computation.2 | async-start | bytes 1638400 | tf_op jit(solution)/shard_map/reduce_scatter | solution.py:142
  94.4 0.7 copy-start.1
  113.7 1.2 copy-start.2
  145.2 27.6 %all-to-all-start = ((f32[8,32,512]{2,1,0:T(8,128)}), f32[8,32,512]{2,1,0:T(8,128)S(1)}, u32[]{:S(2)}, u32[]{:S(2)}) async-start(f32[8,32,512]{2,1,0:T(8,128)} %bitcast.11), calls=%async_computation.1 | async-start | bytes 1048576 | tf_op jit(solution)/shard_map/all_to_all | solution.py:145
  149.8 61.5 %all-gather.8.cloned.1.call-start = ((), (), s32[]{:S(2)}) async-start(), calls=%async_computation.4 | async-start | bytes 2949120 | tf_op jit(solution)/shard_map/all_gather | solution.py:146
Sparse Core Ops, SparseCore 0:
  9.6 84.7 all-gather.5
  115.1 27.8 reduce-scatter.1
  173.9 37.4 all-gather.7
